TPU v7x, 512 devices: a whole 4x8x8 slice. The times are simulated.
512 devices in a mesh: dp: 64 (over z_lo, y, core), mp: 8 (over x, z_hi).
Axes of the slice: x: 4, y: 8, z: 8 (z_hi: 2, z_lo: 4; z = z_hi * 4 + z_lo), core: 2. Of those that a mesh axis runs over, the one named last changes fastest.
Arguments:
- picture_encoder_features: bfloat16 [8192, 6144], P('dp', 'mp'), may hold values from -10 to 10
- caption_encoder_features: bfloat16 [8192, 2048], P('dp', 'mp'), may hold values from -10 to 10
- picture_head_matrix: bfloat16 [6144, 1024], P('mp'), may hold values from -2 to 2
- caption_head_matrix: bfloat16 [2048, 1024], P('mp'), may hold values from -2 to 2
- sharpness_factor: float32 [1], replicated, may hold values from 4 to 8
- offset_shift: float32 [1], replicated, may hold values from -2 to 0
Outputs:
- img_feat_grad: bfloat16 [8192, 6144], P('dp', 'mp')
- txt_feat_grad: bfloat16 [8192, 2048], P('dp', 'mp')
- w_img_grad: float32 [6144, 1024], P(('mp', 'dp'))
- w_txt_grad: float32 [2048, 1024], P(('mp', 'dp'))
All inputs are finite; a program needn't handle non-finite values.
Results may differ from a plain program's by a relative error of at most 0.005.
Values may be sent and summed in bfloat16 or wider, within the bound.
A program may use at most 64 MiB of HBM per device.

v0:
```python
import jax
import jax.numpy as jnp
from jax import lax
from jax.sharding import PartitionSpec as P


def passed_along(block, axis, distance):
    devices = range(lax.axis_size(axis))
    route = [((i - distance) % len(devices), i) for i in devices]
    return lax.ppermute(block, axis, route)


def unit_rows(values):
    scale = lax.rsqrt(jnp.sum(values * values, axis=-1, keepdims=True) + 1e-06)
    return (values * scale, scale)


def back_rows(emb, scale, grad):
    return scale * (grad - emb * jnp.sum(emb * grad, axis=-1, keepdims=True))


def shards(
    picture_encoder_features,
    caption_encoder_features,
    picture_head_matrix,
    caption_head_matrix,
    sharpness_factor,
    offset_shift,
):
    similarity_multiplier = sharpness_factor[0]
    offset_source_index = offset_shift[0]
    groups = lax.axis_size("mp")
    member = lax.axis_index("mp")
    cycle = lax.axis_size("dp")
    place = lax.axis_index("dp")
    rows = picture_encoder_features.shape[0]
    share = rows // groups
    img_z = lax.psum(
        jnp.dot(picture_encoder_features, picture_head_matrix, preferred_element_type=jnp.float32),
        "mp",
    )
    img_emb, img_scale = unit_rows(img_z)
    picture_unit_vectors = img_emb.astype(jnp.bfloat16)
    txt_full = lax.psum(
        jnp.dot(caption_encoder_features, caption_head_matrix, preferred_element_type=jnp.float32),
        "mp",
    )
    txt_z = lax.dynamic_slice_in_dim(txt_full, member * share, share, 0)
    txt_emb, txt_scale = unit_rows(txt_z)
    txt_unit = txt_emb.astype(jnp.bfloat16)
    img_index = place * rows + jnp.arange(rows)

    def tile(tile_piece, source):
        count = tile_piece.shape[0]
        pair_similarities = (
            similarity_multiplier
            * lax.dot_general(
                tile_piece,
                picture_unit_vectors,
                (((1,), (1,)), ((), ())),
                preferred_element_type=jnp.float32,
            )
            + offset_source_index
        )
        txt_index = source * rows + member * share + jnp.arange(count)
        positive = txt_index[:, None] == img_index[None, :]
        sign = jnp.where(positive, jnp.float32(1.0), jnp.float32(-1.0))
        multiplier = (-sign * jax.nn.sigmoid(-sign * pair_similarities)).astype(jnp.bfloat16)
        picture_cost_piece = similarity_multiplier * lax.dot_general(
            multiplier, tile_piece, (((0,), (0,)), ((), ())), preferred_element_type=jnp.float32
        )
        caption_cost_piece = similarity_multiplier * jnp.dot(
            multiplier, picture_unit_vectors, preferred_element_type=jnp.float32
        )
        return (picture_cost_piece, caption_cost_piece)

    picture_running_total = jnp.zeros((rows, picture_unit_vectors.shape[1]), jnp.float32)

    def advance(step, carry):
        tile_piece, grad, image_row_sum = carry
        source = (place - step) % cycle
        picture_cost_piece, caption_cost_piece = tile(tile_piece, source)
        grad = grad + caption_cost_piece
        tile_piece = passed_along(tile_piece, "dp", 1)
        grad = passed_along(grad, "dp", 1)
        return (tile_piece, grad, image_row_sum + picture_cost_piece)

    start_grad = jnp.zeros((share, picture_unit_vectors.shape[1]), jnp.float32)
    tile_piece, caption_derivative, picture_running_total = lax.fori_loop(
        0, cycle, advance, (txt_unit, start_grad, picture_running_total)
    )
    img_grad = lax.psum(picture_running_total, "mp")
    img_cot = back_rows(img_emb, img_scale, img_grad).astype(jnp.bfloat16)
    txt_cot = back_rows(txt_emb, txt_scale, caption_derivative).astype(jnp.bfloat16)
    txt_all = lax.all_gather(txt_cot, "mp", axis=0, tiled=True)
    img_feat_grad = lax.dot_general(
        img_cot, picture_head_matrix, (((1,), (1,)), ((), ())), preferred_element_type=jnp.float32
    ).astype(jnp.bfloat16)
    txt_feat_grad = lax.dot_general(
        txt_all, caption_head_matrix, (((1,), (1,)), ((), ())), preferred_element_type=jnp.float32
    ).astype(jnp.bfloat16)
    w_img_term = (
        lax.dot_general(
            picture_encoder_features,
            img_cot,
            (((0,), (0,)), ((), ())),
            preferred_element_type=jnp.float32,
        )
        / rows
    )
    w_txt_term = (
        lax.dot_general(
            caption_encoder_features,
            txt_all,
            (((0,), (0,)), ((), ())),
            preferred_element_type=jnp.float32,
        )
        / rows
    )
    w_img_grad, w_txt_grad = (
        lax.psum_scatter(w_img_term, "dp", scatter_dimension=0, tiled=True),
        lax.psum_scatter(w_txt_term, "dp", scatter_dimension=0, tiled=True),
    )
    return (img_feat_grad, txt_feat_grad, w_img_grad, w_txt_grad)


def solution(mesh):
    placed = (P("dp", "mp"), P("dp", "mp"), P("mp", None), P("mp", None), P(), P())
    return jax.shard_map(
        shards,
        mesh=mesh,
        in_specs=placed,
        out_specs=(P("dp", "mp"), P("dp", "mp"), P(("mp", "dp"), None), P(("mp", "dp"), None)),
        check_vma=False,
    )
```

profile of v0, /device:TPU:1, one launch (start us, length us, event | category | flops | bytes accessed | tf_op | source)
XLA Modules:
  0.0 1713.5 jit_solution(2500504777761856458)
XLA Ops:
  11.6 142.4 %all-reduce.12.cloned.1.call-done = (f32[128,1024]{1,0:T(8,128)}, f32[128,1024]{1,0:T(8,128)}) async-done(((f32[128,1024]{1,0:T(8,128)}, f32[128,1024]{1,0:T(8,128)}), (f32[128,1024]{1,0:T(8,128)}, f32[128,1024]{1,0:T(8,128)})) %all-reduce.12.cloned.1.call-update) | async-done | bytes 1048592 | tf_op jit(solution)/shard_map/psum | solution.py:44
  158.3 876.8 %while.20 = (s32[]{:T(128)}, bf16[16,1024]{1,0:T(8,128)(2,1)S(1)}, f32[16,1024]{1,0:T(8,128)S(1)}, f32[128,1024]{1,0:T(8,128)S(1)}, f32[]{:T(128)}, /*index=5*/s...) while((s32[]{:T(128)}, bf16[16,1024]{1,0:T(8,128)(2,1)S(1)}, ...), condition=%wide.region_5.6_spmd.clone, body=%wide.region_4.5_spmd.clone.sunk | while | flops 13031585 | bytes 2242064 | solution.py:89
  158.3 5.8 collective-permute-start
  191.3 4.3 collective-permute-done.1
  205.0 4.3 collective-permute-done.1
  218.8 4.3 collective-permute-done.1
  232.6 4.3 collective-permute-done.1
  246.3 4.3 collective-permute-done.1
  260.1 4.3 collective-permute-done.1
  273.8 4.3 collective-permute-done.1
  287.6 4.3 collective-permute-done.1
  301.3 4.3 collective-permute-done.1
  315.1 4.3 collective-permute-done.1
  328.9 4.3 collective-permute-done.1
  342.6 4.3 collective-permute-done.1
  356.4 4.3 collective-permute-done.1
  370.1 4.3 collective-permute-done.1
  383.9 4.3 collective-permute-done.1
  397.6 4.3 collective-permute-done.1
  411.4 4.3 collective-permute-done.1
  425.2 4.3 collective-permute-done.1
  438.9 4.3 collective-permute-done.1
  452.7 4.3 collective-permute-done.1
  466.4 4.3 collective-permute-done.1
  480.2 4.3 collective-permute-done.1
  493.9 4.3 collective-permute-done.1
  507.7 4.3 collective-permute-done.1
  535.2 4.3 collective-permute-done.1
  796.6 4.3 collective-permute-done.1
  1038.0 40.2 %all_gather.3 = bf16[128,1024]{1,0:T(8,128)(2,1)S(1)} all-gather(bf16[16,1024]{1,0:T(8,128)(2,1)S(1)} %multiply_convert_fusion.2), channel_id=1, replica_groups=mesh['dp'=64,'mp'=8] {'mp'}, dimensions={0}, use_global_device_ids=true | all-gather | bytes 294912 | tf_op jit(solution)/shard_map/all_gather | solution.py:95
  1079.4 68.7 %all-reduce.8.cloned.1.call-done = f32[128,1024]{1,0:T(8,128)} async-done(((f32[128,1024]{1,0:T(8,128)}), f32[128,1024]{1,0:T(8,128)}) %all-reduce.8.cloned.1.call-update) | async-done | bytes 524304 | tf_op jit(solution)/shard_map/psum | solution.py:92
  1157.9 545.8 %all-reduce.10.cloned.1.call-done = (f32[768,1024]{0,1:T(8,128)}, f32[256,1024]{0,1:T(8,128)}) async-done(((f32[768,1024]{0,1:T(8,128)}, f32[256,1024]{0,1:T(8,128)}), (f32[768,1024]{0,1:T(8,128)}, f32[256,1024]{0,1:T(8,128)})) %all-reduce.10.cloned.1.call-update) | async-done | bytes 4194320
  (656 shorter events, 777.5 us)
Async XLA Ops:
  7.2 146.9 %all-reduce.12.cloned.1.call-start = ((), (), s32[]{:S(2)}) async-start(), calls=%async_computation.2 | async-start | bytes 2097152 | tf_op jit(solution)/shard_map/psum | solution.py:44
  11.6 1136.6 %all-reduce.8.cloned.1.call-start = ((), (), s32[]{:S(2)}) async-start(), calls=%async_computation | async-start | bytes 1048576 | tf_op jit(solution)/shard_map/psum | solution.py:92
  158.3 11.0 collective-permute-start
  268.7 9.5 collective-permute-start.1
  282.4 9.5 collective-permute-start.1
  296.2 9.5 collective-permute-start.1
  309.9 9.5 collective-permute-start.1
  323.7 9.5 collective-permute-start.1
  406.2 9.5 collective-permute-start.1
  420.0 9.5 collective-permute-start.1
  433.7 9.5 collective-permute-start.1
  447.5 9.5 collective-permute-start.1
  530.0 9.5 collective-permute-start.1
  543.8 9.5 collective-permute-start.1
  557.6 9.5 collective-permute-start.1
  571.3 9.5 collective-permute-start.1
  585.1 9.5 collective-permute-start.1
  667.6 9.5 collective-permute-start.1
  681.4 9.5 collective-permute-start.1
  695.1 9.5 collective-permute-start.1
  708.9 9.5 collective-permute-start.1
  791.4 9.5 collective-permute-start.1
  805.2 9.5 collective-permute-start.1
  818.9 9.5 collective-permute-start.1
  966.0 9.5 collective-permute-start
  970.3 9.6 collective-permute-start.1
  979.8 9.6 collective-permute-start
  984.1 9.6 collective-permute-start.1
  1011.8 9.5 collective-permute-start.1
  1021.3 9.5 collective-permute-start
  1025.6 9.5 collective-permute-start.1
  1035.9 667.7 %all-reduce.10.cloned.1.call-start = ((), (), s32[]{:S(2)}) async-start(), calls=%async_computation.1 | async-start | bytes 8388608
  (106 other events, 2039.4 us)
Sparse Core Ops, SparseCore 0:
  11.7 142.3 all-reduce.11
  1036.1 112.0 all-reduce.7
  1153.1 550.5 all-reduce.9
where the time goes:
time: 1720 us; the launch traced here: 1710 us
  waiting for transfers between devices  1170 us (68%)
  starting transfers between devices  251 us (15%)
  matrix products  216 us (13%)
  blocking collectives  40.2 us (2%)
    unnamed x4, waiting for transfers between devices  546 us
    ppermute x128, waiting for transfers between devices, passed_along(): return lax.ppermute(block, axis, route)  414 us
    ppermute x128, starting transfers between devices, passed_along(): return lax.ppermute(block, axis, route)  251 us
    psum x1, waiting for transfers between devices, shards(): lax.psum(jnp.dot(caption_encoder_features, caption_head_matrix, preferred...  142 us
    dot_general x64, matrix products, tile(): lax.dot_general(tile_piece, picture_unit_vectors, (((1,), (1,)), ((), ())...  94.9 us
    psum x1, waiting for transfers between devices, shards(): img_grad = lax.psum(picture_running_total, 'mp')  68.7 us
    dot_general x64, matrix products, tile(): lax.dot_general(multiplier, tile_piece, (((0,), (0,)), ((), ())), preferr...  59.6 us
    dot_general x64, matrix products, tile(): jnp.dot(multiplier, picture_unit_vectors, preferred_element_type=jnp.floa...  51.5 us
  transfers between devices with their start and end apart: 131, of which 129 were waited for; matrix products, arithmetic and copies ran while one was open for 12% of the time, Pallas kernels for 0%

commit v1 on v0

v1 whole, which is shorter than its diff:
```python
import jax
import jax.numpy as jnp
from jax import lax
from jax.sharding import PartitionSpec as P


def unit_rows(values):
    scale = lax.rsqrt(jnp.sum(values * values, axis=-1, keepdims=True) + 1e-06)
    return (values * scale, scale)


def back_rows(emb, scale, grad):
    return scale * (grad - emb * jnp.sum(emb * grad, axis=-1, keepdims=True))


def dot(a, b, dims):
    return lax.dot_general(a, b, (dims, ((), ())), preferred_element_type=jnp.float32)


def shards(img_x, txt_x, img_w, txt_w, sharpness_factor, offset_shift):
    sharp = sharpness_factor[0]
    offset = offset_shift[0]
    groups = lax.axis_size("mp")
    member = lax.axis_index("mp")
    cycle = lax.axis_size("dp")
    place = lax.axis_index("dp")
    rows = img_x.shape[0]
    share = rows // groups
    width = img_w.shape[1]
    z_img = dot(img_x, img_w, ((1,), (0,))).reshape(groups, share, width)
    z_txt = dot(txt_x, txt_w, ((1,), (0,))).reshape(groups, share, width)
    z = lax.psum_scatter(
        jnp.concatenate([z_img, z_txt], axis=1), "mp", scatter_dimension=0, tiled=True
    )[0]
    emb, scale = unit_rows(z)
    unit = emb.astype(jnp.bfloat16)
    img_unit = lax.all_gather(unit[:share], "mp", axis=0, tiled=True)
    txt_unit = lax.all_gather(unit[share:], "dp", axis=0, tiled=True)
    logits = sharp * dot(txt_unit, img_unit, ((1,), (1,))) + offset
    t = jnp.arange(cycle * share)
    txt_index = (t // share) * rows + member * share + t % share
    img_index = place * rows + jnp.arange(rows)
    sign = jnp.where(txt_index[:, None] == img_index[None, :], 1.0, -1.0).astype(jnp.float32)
    coef = (-sign * jax.nn.sigmoid(-sign * logits)).astype(jnp.bfloat16)
    img_part = dot(coef, txt_unit, ((0,), (0,)))
    txt_part = dot(coef, img_unit, ((1,), (0,)))
    txt_grad = lax.psum_scatter(txt_part, "dp", scatter_dimension=0, tiled=True)
    img_grad = lax.psum_scatter(img_part, "mp", scatter_dimension=0, tiled=True)
    grad = sharp * jnp.concatenate([img_grad, txt_grad], axis=0)
    cot = back_rows(emb, scale, grad).astype(jnp.bfloat16)
    cots = lax.all_gather(cot, "mp", axis=0)
    img_cot = cots[:, :share].reshape(rows, width)
    txt_cot = cots[:, share:].reshape(rows, width)
    img_feat_grad = dot(img_cot, img_w, ((1,), (1,))).astype(jnp.bfloat16)
    txt_feat_grad = dot(txt_cot, txt_w, ((1,), (1,))).astype(jnp.bfloat16)
    w_img = (dot(img_x, img_cot, ((0,), (0,))) / rows).reshape(cycle, -1, width)
    w_txt = (dot(txt_x, txt_cot, ((0,), (0,))) / rows).reshape(cycle, -1, width)
    n_img = w_img.shape[1]
    w = lax.psum_scatter(
        jnp.concatenate([w_img, w_txt], axis=1), "dp", scatter_dimension=0, tiled=True
    )[0]
    return (img_feat_grad, txt_feat_grad, w[:n_img], w[n_img:])


def solution(mesh):
    placed = (P("dp", "mp"), P("dp", "mp"), P("mp", None), P("mp", None), P(), P())
    return jax.shard_map(
        shards,
        mesh=mesh,
        in_specs=placed,
        out_specs=(P("dp", "mp"), P("dp", "mp"), P(("mp", "dp"), None), P(("mp", "dp"), None)),
        check_vma=False,
    )
```

time: 1720 us -> 957 us (0.56)
  waiting for transfers between devices: 1170 us -> 823 us
  starting transfers between devices: 251 us -> 0.21 us
  matrix products: 216 us -> 13.8 us
  blocking collectives: 40.2 us -> 78 us
    reduce_scatter x0 -> x4, waiting for transfers between devices: none -> 746 us  [the longest x1 282 us: shards(): txt_grad = lax.psum_scatter(txt_part, 'dp', scatter_dimension=0, tiled=True)]
    unnamed x4 -> x5, waiting for transfers between devices: 546 us -> 0.08 us
    ppermute x128 -> x0, waiting for transfers between devices: 414 us -> none  [passed_along(): return lax.ppermute(block, axis, route)]
    ppermute x128 -> x0, starting transfers between devices: 251 us -> none  [passed_along(): return lax.ppermute(block, axis, route)]
    psum x2 -> x0, waiting for transfers between devices: 211 us -> none  [the longest x1 142 us: shards(): lax.psum(jnp.dot(caption_encoder_features, caption_head_matrix, preferred...]
    dot_general x198 -> x9, matrix products: 216 us -> 13.8 us  [dot(): lax.dot_general(a, b, (dims, ((), ())), preferred_element_type=jnp.float32)]
    all_gather x0 -> x1, waiting for transfers between devices: none -> 76.4 us  [shards(): txt_unit = lax.all_gather(unit[share:], 'dp', axis=0, tiled=True)]
    all_gather x1 -> x2, blocking collectives: 40.2 us -> 78 us  [the longest x1 39.6 us: shards(): cots = lax.all_gather(cot, 'mp', axis=0)]
  transfers between devices with their start and end apart: 131 -> 5, of which waited for: 129 -> 5; matrix products, arithmetic and copies ran while one was open for 12% -> 1% of each run, Pallas kernels for 0% -> 0%
where the time goes in v1:
time: 957 us; the launch traced here: 952 us
  waiting for transfers between devices  823 us (86%)
  blocking collectives  78 us (8%)
  between operations  15.2 us (2%)
  matrix products  13.8 us (1%)
  local copies, waits for them, and re-layouts  12 us (1%)
  other arithmetic  10 us (1%)
    reduce_scatter x1, waiting for transfers between devices, shards(): txt_grad = lax.psum_scatter(txt_part, 'dp', scatter_dimension=0, tiled=True)  282 us
    reduce_scatter x1, waiting for transfers between devices, shards(): lax.psum_scatter(jnp.concatenate([w_img, w_txt], axis=1), 'dp', scatter_d...  282 us
    reduce_scatter x1, waiting for transfers between devices, shards(): lax.psum_scatter(jnp.concatenate([z_img, z_txt], axis=1), 'mp', scatter_d...  98.5 us
    reduce_scatter x1, waiting for transfers between devices, shards(): img_grad = lax.psum_scatter(img_part, 'mp', scatter_dimension=0, tiled=True)  83.9 us
    all_gather x1, waiting for transfers between devices, shards(): txt_unit = lax.all_gather(unit[share:], 'dp', axis=0, tiled=True)  76.4 us
    all_gather x1, blocking collectives, shards(): cots = lax.all_gather(cot, 'mp', axis=0)  39.6 us
    all_gather x1, blocking collectives, shards(): img_unit = lax.all_gather(unit[:share], 'mp', axis=0, tiled=True)  38.4 us
  transfers between devices with their start and end apart: 5, of which 5 were waited for; matrix products, arithmetic and copies ran while one was open for 1% of the time, Pallas kernels for 0%

profile of v1, /device:TPU:1, one launch (start us, length us, event | category | flops | bytes accessed | tf_op | source)
XLA Modules:
  0.0 952.1 jit_solution(11934852567903240409)
XLA Ops:
  7.2 1.3 copy-done
  8.6 1.3 fusion.28
  9.9 0.2 fusion.29
  10.1 1.0 pad_maximum_fusion.1
  11.2 0.0 all-gather.2.cloned.1.call-start
  11.3 98.5 %reduce-scatter.5.cloned.1.call-done = f32[1,32,1024]{2,1,0:T(8,128)} async-done(((f32[8,32,1024]{2,1,0:T(8,128)}), f32[1,32,1024]{2,1,0:T(8,128)}) %reduce-scatter.5.cloned.1.call-update) | async-done | bytes 131088 | tf_op jit(solution)/shard_map/reduce_scatter | solution.py:32
  109.7 1.0 fusion.14
  110.8 1.0 fusion.15
  111.8 0.6 fusion.27
  112.4 0.0 reduce-scatter.7.cloned.1.call-start
  113.8 38.4 %all_gather.11 = bf16[128,1024]{1,0:T(8,128)(2,1)S(1)} all-gather(bf16[16,1024]{1,0:T(8,128)(2,1)S(1)} %get-tuple-element.6), channel_id=1, replica_groups=mesh['dp'=64,'mp'=8] {'mp'}, dimensions={0}, use_global_device_ids=true | all-gather | bytes 294912 | tf_op jit(solution)/shard_map/all_gather | solution.py:37
  152.2 76.4 %all-gather.2.cloned.1.call-done = bf16[1024,1024]{1,0:T(8,128)(2,1)} async-done(((bf16[16,1024]{1,0:T(8,128)(2,1)}), bf16[1024,1024]{1,0:T(8,128)(2,1)}) %all-gather.2.cloned.1.call-update) | async-done | bytes 2097168 | tf_op jit(solution)/shard_map/all_gather | solution.py:38
  228.6 2.5 fusion.8
  231.1 1.3 fusion.30
  232.4 0.0 reduce-scatter.9.cloned.1.call-start
  232.4 2.6 fusion.31
  235.2 83.9 %reduce-scatter.7.cloned.1.call-done = f32[16,1024]{1,0:T(8,128)} async-done(((f32[128,1024]{1,0:T(8,128)}), f32[16,1024]{1,0:T(8,128)}) %reduce-scatter.7.cloned.1.call-update) | async-done | bytes 65552 | tf_op jit(solution)/shard_map/reduce_scatter | solution.py:48
  319.0 282.3 %reduce-scatter.9.cloned.1.call-done = f32[16,1024]{1,0:T(8,128)} async-done(((f32[1024,1024]{1,0:T(8,128)}), f32[16,1024]{1,0:T(8,128)}) %reduce-scatter.9.cloned.1.call-update) | async-done | bytes 65552 | tf_op jit(solution)/shard_map/reduce_scatter | solution.py:47
  601.3 1.1 fusion.13
  602.4 1.0 fusion.11
  603.3 39.6 %all_gather.12 = bf16[8,32,1024]{2,1,0:T(8,128)(2,1)S(1)} all-gather(bf16[1,32,1024]{2,1,0:T(8,128)(2,1)S(1)} %fusion.11), channel_id=1, replica_groups=mesh['dp'=64,'mp'=8] {'mp'}, dimensions={0}, use_global_device_ids=true | all-gather | bytes 589824 | tf_op jit(solution)/shard_map/all_gather | solution.py:51
  642.9 1.3 fusion
  644.3 1.5 reshape.115
  645.8 2.3 multiply_bitcast_fusion
  648.1 4.6 reshape.114
  652.7 4.9 pad_maximum_fusion
  657.6 1.0 copy-done.4
  658.6 0.9 convolution_convert_fusion.1
  659.6 1.3 convolution_convert_fusion
  660.9 281.8 %reduce-scatter.11.cloned.1.call-done = f32[1,16,1024]{2,1,0:T(8,128)} async-done(((f32[64,16,1024]{2,1,0:T(8,128)}), f32[1,16,1024]{2,1,0:T(8,128)}) %reduce-scatter.11.cloned.1.call-update) | async-done | bytes 65552 | tf_op jit(solution)/shard_map/reduce_scatter | solution.py:59
  942.7 1.4 slice_bitcast_fusion.1
  944.1 1.5 slice_bitcast_fusion
  (23 shorter events, 0.3 us)
Async XLA Ops:
  7.2 1.4 copy-start
  7.2 2.7 copy-start.3
  7.2 2.7 copy-start.6
  7.2 102.5 %reduce-scatter.5.cloned.1.call-start = ((), (), s32[]{:S(2)}) async-start(), calls=%async_computation.4 | async-start | bytes 1179648 | tf_op jit(solution)/shard_map/reduce_scatter | solution.py:32
  11.2 217.4 %all-gather.2.cloned.1.call-start = ((), (), s32[]{:S(2)}) async-start(), calls=%async_computation.5 | async-start | bytes 2129920 | tf_op jit(solution)/shard_map/all_gather | solution.py:38
  112.4 206.6 %reduce-scatter.7.cloned.1.call-start = ((), (), s32[]{:S(2)}) async-start(), calls=%async_computation.6 | async-start | bytes 589824 | tf_op jit(solution)/shard_map/reduce_scatter | solution.py:48
  228.6 2.5 copy-start.2
  232.4 368.9 %reduce-scatter.9.cloned.1.call-start = ((), (), s32[]{:S(2)}) async-start(), calls=%async_computation.7 | async-start | bytes 4259840 | tf_op jit(solution)/shard_map/reduce_scatter | solution.py:47
  235.1 366.2 %copy-start.1 = (f32[1,32,1024]{2,1,0:T(8,128)S(1)}, f32[1,32,1024]{2,1,0:T(8,128)}, u32[]{:S(2)}) copy-start(f32[1,32,1024]{2,1,0:T(8,128)} %reduce-scatter.5.cloned.1.call-done) | copy-start | bytes 393220
  235.1 707.6 %reduce-scatter.11.cloned.1.call-start = ((), (), s32[]{:S(2)}) async-start(), calls=%async_computation.8 | async-start | bytes 4259840 | tf_op jit(solution)/shard_map/reduce_scatter | solution.py:59
  642.9 2.9 copy-start.5
  657.6 1.0 copy-start.4
Sparse Core Ops, SparseCore 0:
  12.5 97.1 reduce-scatter.4
  112.7 115.8 all-gather.1
  233.7 85.2 reduce-scatter.6
  321.7 279.5 reduce-scatter.8
  657.7 284.9 reduce-scatter.10
